TPU v7x, 256 devices: a whole 4x4x8 slice. The times are simulated.
256 devices in a mesh: grp: 8 (over x, y_hi), seq: 32 (over z, y_lo, core).
Axes of the slice: x: 4, y: 4 (y_hi: 2, y_lo: 2; y = y_hi * 2 + y_lo), z: 8, core: 2. Of those that a mesh axis runs over, the one named last changes fastest.
Arguments:
- query_rows: bfloat16 [49152, 2048], P(('grp', 'seq')), may hold values from -150 to 150
- key_rows: bfloat16 [49152, 2048], P(('grp', 'seq')), may hold values from -5 to 5
- value_rows: bfloat16 [49152, 2048], P(('grp', 'seq')), may hold values from -6 to 6
- cotangent: bfloat16 [49152, 2048], P(('grp', 'seq')), may hold values from -6 to 6
- partner: int32 [8, 32], P('grp'), may hold values from 0 to 31, each once within a row
- anchors: int32 [8], P('grp'), may hold values from 0 to 31
- global_list: int32 [256, 2], P(('grp', 'seq')), may hold values from 0 to 2, as said below
Outputs:
- attended: bfloat16 [49152, 2048], P(('grp', 'seq'))
- grad_queries: bfloat16 [49152, 2048], P(('grp', 'seq'))
- grad_keys: bfloat16 [49152, 2048], P(('grp', 'seq'))
- grad_values: bfloat16 [49152, 2048], P(('grp', 'seq'))
Inputs may be any that keep to these rules, and one draw needn't show every extreme that they name: `global_list`: each row lists distinct offsets of 1 to 2 first and zeros after them; offset d in the row of block 32 g + s names the global block of segment (g - d) mod 8.
All inputs are finite; a program needn't handle non-finite values.
Results may differ from a plain program's by a relative error of at most 0.022.
Values may be sent and summed in bfloat16 or wider, within the bound.
A program may use at most 192 MiB of HBM per device.

v0:
```python
import jax
import jax.numpy as jnp
from jax import lax
from jax.sharding import PartitionSpec as P

HEAD_DIM = 128
GLOBALS = 2


def broadcast(value, axis, source):
    kept = jnp.where(lax.axis_index(axis) == source, value, 0).astype(value.dtype)
    return lax.psum(kept, axis)


def passed_along(block, axis, distance):
    devices = range(lax.axis_size(axis))
    route = [((i - distance) % len(devices), i) for i in devices]
    return lax.ppermute(block, axis, route)


def attend_block(query_block, key_set, value_set, live_mask, grad_block):
    heads_here = query_block.shape[1] // HEAD_DIM
    scaling = HEAD_DIM ** (-0.5)
    query_heads = query_block.reshape(-1, heads_here, HEAD_DIM)
    key_heads = key_set.reshape(-1, heads_here, HEAD_DIM)
    value_heads = value_set.reshape(-1, heads_here, HEAD_DIM)
    grad_heads = grad_block.reshape(-1, heads_here, HEAD_DIM)
    offset_row = jnp.where(live_mask, 0.0, -jnp.inf).astype(jnp.float32)
    scores = (
        jnp.einsum("qhd,khd->hqk", query_heads, key_heads, preferred_element_type=jnp.float32)
        * scaling
        + offset_row[None, None, :]
    )
    row_top = jnp.max(scores, axis=-1, keepdims=True)
    lifted = jnp.exp(scores - row_top)
    probs = lifted / jnp.sum(lifted, axis=-1, keepdims=True)
    weights = probs.astype(jnp.bfloat16)
    width_all = query_block.shape[1]
    attended = (
        jnp.einsum("hqk,khd->qhd", weights, value_heads, preferred_element_type=jnp.float32)
        .reshape(-1, width_all)
        .astype(jnp.bfloat16)
    )
    dprob = jnp.einsum("qhd,khd->hqk", grad_heads, value_heads, preferred_element_type=jnp.float32)
    delta = jnp.sum(probs * dprob, axis=-1, keepdims=True)
    dscore = (probs * (dprob - delta)).astype(jnp.bfloat16)
    grad_query = (
        (
            jnp.einsum("hqk,khd->qhd", dscore, key_heads, preferred_element_type=jnp.float32)
            * scaling
        )
        .reshape(-1, width_all)
        .astype(jnp.bfloat16)
    )
    key_terms = (
        jnp.einsum("hqk,qhd->khd", dscore, query_heads, preferred_element_type=jnp.float32)
        * scaling
    ).reshape(-1, width_all)
    value_terms = jnp.einsum(
        "hqk,qhd->khd", weights, grad_heads, preferred_element_type=jnp.float32
    ).reshape(-1, width_all)
    return (attended, grad_query, key_terms, value_terms)


def on_device(query_rows, key_rows, value_rows, cotangent, partner, anchors, global_list):
    seq_count = lax.axis_size("seq")
    block_rows, width_all = query_rows.shape
    sorting = partner[0]
    anchor_seat = anchors[0]
    packed = jnp.concatenate([key_rows, value_rows], 1)
    spread = lax.all_to_all(
        packed.reshape(1, block_rows, 2 * width_all), "seq", split_axis=1, concat_axis=0, tiled=True
    )
    chosen = jnp.take(spread, sorting, axis=0)
    partner_kv = lax.all_to_all(chosen, "seq", split_axis=0, concat_axis=1, tiled=True).reshape(
        block_rows, 2 * width_all
    )
    anchor_block = broadcast(packed, "seq", anchor_seat)
    assembled = jnp.stack(
        [passed_along(anchor_block, "grp", offset) for offset in range(1, GLOBALS + 1)]
    )
    every_kv = jnp.concatenate(
        [packed, partner_kv, assembled.reshape(GLOBALS * block_rows, 2 * width_all)], 0
    )
    listed = [jnp.any(global_list[0] == offset) for offset in range(1, GLOBALS + 1)]
    live_mask = jnp.concatenate(
        [jnp.ones((2 * block_rows,), bool)]
        + [jnp.broadcast_to(flag, (block_rows,)) for flag in listed]
    )
    attended, grad_query, key_terms, value_terms = attend_block(
        query_rows, every_kv[:, :width_all], every_kv[:, width_all:], live_mask, cotangent
    )
    key_terms = key_terms.reshape(2 + GLOBALS, block_rows, width_all)
    value_terms = value_terms.reshape(2 + GLOBALS, block_rows, width_all)
    partner_terms = jnp.concatenate([key_terms[1], value_terms[1]], 1).astype(jnp.bfloat16)
    spread_back = lax.all_to_all(
        partner_terms.reshape(1, block_rows, 2 * width_all),
        "seq",
        split_axis=1,
        concat_axis=0,
        tiled=True,
    )
    seats = jnp.arange(seq_count, dtype=jnp.int32)
    inverse = jnp.sum(jnp.where(sorting[:, None] == seats[None, :], seats[:, None], 0), 0)
    placed = jnp.take(spread_back, inverse, axis=0)
    returned = lax.all_to_all(placed, "seq", split_axis=0, concat_axis=1, tiled=True).reshape(
        block_rows, 2 * width_all
    )
    global_terms = [
        jnp.concatenate([key_terms[1 + offset], value_terms[1 + offset]], 1).astype(jnp.bfloat16)
        for offset in range(1, GLOBALS + 1)
    ]
    back_sum = jnp.zeros((block_rows, 2 * width_all), jnp.float32)
    for offset in range(1, GLOBALS + 1):
        back_sum = back_sum + passed_along(global_terms[offset - 1], "grp", -offset).astype(
            jnp.float32
        )
    anchor_total = lax.psum(back_sum.astype(jnp.bfloat16), "seq").astype(jnp.float32)
    is_anchor = (lax.axis_index("seq") == anchor_seat).astype(jnp.float32)
    grad_kv = (
        jnp.concatenate([key_terms[0], value_terms[0]], 1)
        + returned.astype(jnp.float32)
        + is_anchor * anchor_total
    )
    return (
        attended,
        grad_query,
        grad_kv[:, :width_all].astype(jnp.bfloat16),
        grad_kv[:, width_all:].astype(jnp.bfloat16),
    )


def solution(mesh):
    placed = (
        P(("grp", "seq"), None),
        P(("grp", "seq"), None),
        P(("grp", "seq"), None),
        P(("grp", "seq"), None),
        P("grp", None),
        P("grp"),
        P(("grp", "seq"), None),
    )
    return jax.shard_map(
        on_device,
        mesh=mesh,
        in_specs=placed,
        out_specs=(
            P(("grp", "seq"), None),
            P(("grp", "seq"), None),
            P(("grp", "seq"), None),
            P(("grp", "seq"), None),
        ),
        check_vma=False,
    )
```

profile of v0, /device:TPU:1, one launch (start us, length us, event | category | flops | bytes accessed | tf_op | source)
XLA Modules:
  0.0 785.9 jit_solution(3919421595357997124)
XLA Ops:
  9.6 5.2 copy.169
  15.4 13.1 %reduce.6 = bf16[192,4096]{1,0:T(8,128)(2,1)} reduce(bf16[192,1,4096]{2,1,0:T(2,128)(2,1)} %bitcast.142, bf16[]{:T(256)} %broadcast.57), dimensions={1}, to_apply=%bitcast.137.reduce_sub_computation | reduce | bytes 3145730
  28.4 4.6 reshape.158
  33.0 11.2 %all-to-all-start = ((bf16[32,2,12288]{2,1,0:T(2,128)(2,1)}), bf16[32,2,12288]{2,1,0:T(2,128)(2,1)}, u32[]{:S(2)}, u32[]{:S(2)}) async-start(bf16[32,2,12288]{2,1,0:T(2,128)(2,1)} %reshape.158), calls=%async_computation | async-start | bytes 3145728 | tf_op jit(solution)/shard_map/all_to_all | solution.py:71
  46.4 37.1 %all-to-all-done = bf16[32,2,12288]{2,1,0:T(2,128)(2,1)} async-done(((bf16[32,2,12288]{2,1,0:T(2,128)(2,1)}), bf16[32,2,12288]{2,1,0:T(2,128)(2,1)}, u32[]{:S(2)}, u32[]{:S(2)}) %all-to-all-start) | async-done | bytes 1572896 | tf_op jit(solution)/shard_map/all_to_all | solution.py:71
  83.5 9.5 %reshape.159 = bf16[192,1,4096]{2,1,0:T(2,128)(2,1)} reshape(bf16[32,2,12288]{2,1,0:T(2,128)(2,1)} %all-to-all-done) | data formatting | bytes 3145728
  92.9 12.5 %bitcast_reduce_fusion.2 = bf16[192,4096]{1,0:T(8,128)(2,1)} fusion(bf16[192,1,4096]{2,1,0:T(2,128)(2,1)} %reshape.159), kind=kLoop, calls=%fused_computation.84 | loop fusion | bytes 3145728 | tf_op jit(solution)/shard_map/all_to_all | solution.py:71
  108.9 3.6 gather_fusion
  115.8 6.3 all-to-all-start.1
  122.1 175.0 %all-reduce.3.cloned.1.call-done = bf16[192,4096]{1,0:T(8,128)(2,1)} async-done(((bf16[192,4096]{1,0:T(8,128)(2,1)}), bf16[192,4096]{1,0:T(8,128)(2,1)}) %all-reduce.3.cloned.1.call-update) | async-done | bytes 1572880 | tf_op jit(solution)/shard_map/psum | solution.py:12
  302.6 31.8 %collective-permute-done.1 = bf16[192,4096]{1,0:T(8,128)(2,1)S(1)} collective-permute-done((bf16[192,4096]{1,0:T(8,128)(2,1)}, bf16[192,4096]{1,0:T(8,128)(2,1)S(1)}, u32[]{:S(2)}, u32[]{:S(2)}) %collective-permute-start.1) | collective-permute-done | bytes 1572896 | tf_op jit(solution)/shard_map/ppermute | solution.py:18
  334.4 35.5 %collective-permute-done = bf16[192,4096]{1,0:T(8,128)(2,1)S(1)} collective-permute-done((bf16[192,4096]{1,0:T(8,128)(2,1)}, bf16[192,4096]{1,0:T(8,128)(2,1)S(1)}, u32[]{:S(2)}, u32[]{:S(2)}) %collective-permute-start) | collective-permute-done | bytes 1572896 | tf_op jit(solution)/shard_map/ppermute | solution.py:18
  371.8 3.7 reshape.127
  382.2 4.7 copy.82
  386.9 4.8 copy.81
  391.6 8.5 %fusion.45 = (f32[16,192]{1,0:T(8,128)S(1)}, f32[16,192,768]{2,1,0:T(8,128)}) fusion(f32[768]{0:T(1024)S(1)} %add_select_fusion, bf16[768,16,128]{0,2,1:T(8,128)(2,1)} %bitcast.140, bf16[192,2048]{1,0:T(8,128)(2,1)S(1)} %copy-done.8), kind=kOutput, calls=%fused_computation.80 | convolution fusion | flops 613417728 | bytes 13384704 | tf_op jit(solution)/shard_map/sub | solution.py:35
  400.2 10.1 %fusion.50 = (bf16[768,16,128]{2,0,1:T(8,128)(2,1)}, f32[768,16,128]{2,0,1:T(8,128)}) fusion(f32[16,192,768]{2,1,0:T(8,128)} %get-tuple-element.18, f32[16,192]{1,0:T(8,128)S(1)} %get-tuple-element.17, bf16[192,2048]{1,0:T(8,128)(2,1)S(1)} %copy-done), kind=kOutput, calls=%fused_computation.81 | convolution fusion | flops 610271232 | bytes 19673088 | tf_op jit(solution)/shard_map/hqk,qhd->khd/dot_general | solution.py:59
  410.2 4.5 fusion.1
  415.8 7.5 fusion.3
  423.3 4.7 fusion.51
  432.3 5.2 copy.168
  437.5 12.0 %reduce.7 = bf16[192,4096]{1,0:T(8,128)(2,1)S(1)} reduce(bf16[192,1,4096]{2,1,0:T(2,128)(2,1)} %bitcast.143, bf16[]{:T(256)} %broadcast.57), dimensions={1}, to_apply=%bitcast.136.reduce_sub_computation | reduce | bytes 3145730
  451.8 5.4 all-to-all-start.2
  462.8 33.5 %all-to-all-done.2 = bf16[32,2,12288]{2,1,0:T(2,128)(2,1)S(1)} async-done(((bf16[32,2,12288]{2,1,0:T(2,128)(2,1)}), bf16[32,2,12288]{2,1,0:T(2,128)(2,1)S(1)}, u32[]{:S(2)}, u32[]{:S(2)}) %all-to-all-start.2) | async-done | bytes 1572896 | tf_op jit(solution)/shard_map/all_to_all | solution.py:96
  496.3 4.1 reshape.161
  500.5 12.5 %bitcast_reduce_fusion.1 = bf16[192,4096]{1,0:T(8,128)(2,1)} fusion(bf16[192,1,4096]{2,1,0:T(2,128)(2,1)} %reshape.161), kind=kLoop, calls=%fused_computation.83 | loop fusion | bytes 3145728 | tf_op jit(solution)/shard_map/all_to_all | solution.py:96
  520.5 4.5 all-to-all-start.3
  525.4 6.1 fusion.19
  536.1 4.7 fusion.18
  547.4 27.9 %all-to-all-done.3 = bf16[32,6,4096]{2,1,0:T(8,128)(2,1)S(1)} async-done(((bf16[32,6,4096]{2,1,0:T(8,128)(2,1)}), bf16[32,6,4096]{2,1,0:T(8,128)(2,1)S(1)}, u32[]{:S(2)}, u32[]{:S(2)}) %all-to-all-start.3) | async-done | bytes 1572896 | tf_op jit(solution)/shard_map/all_to_all | solution.py:106
  577.2 196.1 %all-reduce.5.cloned.1.call-done = bf16[192,4096]{1,0:T(8,128)(2,1)} async-done(((bf16[192,4096]{1,0:T(8,128)(2,1)}), bf16[192,4096]{1,0:T(8,128)(2,1)}) %all-reduce.5.cloned.1.call-update) | async-done | bytes 1572880 | tf_op jit(solution)/shard_map/psum | solution.py:118
  773.3 4.0 fusion.11
  (79 shorter events, 60.6 us)
Async XLA Ops:
  7.2 393.0 %copy-start = (bf16[192,2048]{1,0:T(8,128)(2,1)S(1)}, bf16[192,2048]{1,0:T(8,128)(2,1)}, u32[]{:S(2)}) copy-start(bf16[192,2048]{1,0:T(8,128)(2,1)} %param.12) | copy-start | bytes 2359300
  33.0 50.4 %all-to-all-start = ((bf16[32,2,12288]{2,1,0:T(2,128)(2,1)}), bf16[32,2,12288]{2,1,0:T(2,128)(2,1)}, u32[]{:S(2)}, u32[]{:S(2)}) async-start(bf16[32,2,12288]{2,1,0:T(2,128)(2,1)} %reshape.158), calls=%async_computation | async-start | bytes 3145728 | tf_op jit(solution)/shard_map/all_to_all | solution.py:71
  44.2 2.0 copy-start.10
  44.2 252.9 %all-reduce.3.cloned.1.call-start = ((), (), s32[]{:S(2)}) async-start(), calls=%async_computation.4 | async-start | bytes 3145728 | tf_op jit(solution)/shard_map/psum | solution.py:12
  115.8 184.7 %copy-start.11 = (s32[1,2]{1,0:T(1,128)S(1)}, s32[1,2]{1,0:T(1,128)}, u32[]{:S(2)}) copy-start(s32[1,2]{1,0:T(1,128)} %param.15) | copy-start | bytes 28
  115.8 256.0 %all-to-all-start.1 = ((bf16[32,6,4096]{2,1,0:T(8,128)(2,1)}), bf16[32,6,4096]{2,1,0:T(8,128)(2,1)}, u32[]{:S(2)}, u32[]{:S(2)}) async-start(bf16[32,6,4096]{2,1,0:T(8,128)(2,1)} %broadcast_select_fusion.1), calls=%async_computation.1 | async-start | bytes 4194304 | tf_op jit(solution)/shard_map/all_to_all | solution.py:75
  297.1 37.3 %collective-permute-start.1 = (bf16[192,4096]{1,0:T(8,128)(2,1)}, bf16[192,4096]{1,0:T(8,128)(2,1)S(1)}, u32[]{:S(2)}, u32[]{:S(2)}) collective-permute-start(bf16[192,4096]{1,0:T(8,128)(2,1)} %all-reduce.3.cloned.1.call-done), channel_id=1, source_target_pairs={{192,0},{224,32},{0,64},{32,96},{64,128},{96,160},{128,192},{160,2... | collective-permute-start | bytes 4718600 | tf_op jit(solution)/shard_map/ppermute | solution.py:18
  298.3 71.6 %collective-permute-start = (bf16[192,4096]{1,0:T(8,128)(2,1)}, bf16[192,4096]{1,0:T(8,128)(2,1)S(1)}, u32[]{:S(2)}, u32[]{:S(2)}) collective-permute-start(bf16[192,4096]{1,0:T(8,128)(2,1)} %all-reduce.3.cloned.1.call-done), channel_id=1, source_target_pairs={{224,0},{0,32},{32,64},{64,96},{96,128},{128,160},{160,192},{192,2... | collective-permute-start | bytes 4718600 | tf_op jit(solution)/shard_map/ppermute | solution.py:18
  386.9 4.8 copy-start.8
  400.2 10.1 %copy-start.3 = (f32[16,192,768]{2,1,0:T(8,128)S(1)}, f32[16,192,768]{2,1,0:T(8,128)}, u32[]{:S(2)}) copy-start(f32[16,192,768]{2,1,0:T(8,128)} %get-tuple-element.18) | copy-start | bytes 28311556
  400.2 10.1 %copy-start.6 = (bf16[768,2048]{0,1:T(8,128)(2,1)S(1)}, bf16[768,2048]{0,1:T(8,128)(2,1)}, u32[]{:S(2)}) copy-start(bf16[768,2048]{0,1:T(8,128)(2,1)} %copy.81) | copy-start | bytes 9437188
  410.2 4.5 copy-start.7
  415.7 7.5 copy-start.9
  423.3 4.7 copy-start.2
  451.8 44.5 %all-to-all-start.2 = ((bf16[32,2,12288]{2,1,0:T(2,128)(2,1)}), bf16[32,2,12288]{2,1,0:T(2,128)(2,1)S(1)}, u32[]{:S(2)}, u32[]{:S(2)}) async-start(bf16[32,2,12288]{2,1,0:T(2,128)(2,1)} %reshape.160), calls=%async_computation.2 | async-start | bytes 3145728 | tf_op jit(solution)/shard_map/all_to_all | solution.py:96
  457.1 1.1 copy-start.5
  457.1 1.4 copy-start.4
  460.0 72.6 %collective-permute-start.3 = (bf16[192,4096]{1,0:T(8,128)(2,1)}, bf16[192,4096]{1,0:T(8,128)(2,1)}, u32[]{:S(2)}, u32[]{:S(2)}) collective-permute-start(bf16[192,4096]{1,0:T(8,128)(2,1)} %pad_maximum_fusion.4), channel_id=1, source_target_pairs={{64,0},{96,32},{128,64},{160,96},{192,128},{224,160},{0,192},{32,2... | collective-permute-start | bytes 4718600 | tf_op jit(solution)/shard_map/ppermute | solution.py:18
  462.5 70.0 %collective-permute-start.2 = (bf16[192,4096]{1,0:T(8,128)(2,1)}, bf16[192,4096]{1,0:T(8,128)(2,1)}, u32[]{:S(2)}, u32[]{:S(2)}) collective-permute-start(bf16[192,4096]{1,0:T(8,128)(2,1)} %pad_maximum_fusion.3), channel_id=1, source_target_pairs={{32,0},{64,32},{96,64},{128,96},{160,128},{192,160},{224,192},{0,2... | collective-permute-start | bytes 4718600 | tf_op jit(solution)/shard_map/ppermute | solution.py:18
  520.5 54.8 %all-to-all-start.3 = ((bf16[32,6,4096]{2,1,0:T(8,128)(2,1)}), bf16[32,6,4096]{2,1,0:T(8,128)(2,1)S(1)}, u32[]{:S(2)}, u32[]{:S(2)}) async-start(bf16[32,6,4096]{2,1,0:T(8,128)(2,1)} %broadcast_select_fusion), calls=%async_computation.3 | async-start | bytes 4194304 | tf_op jit(solution)/shard_map/all_to_all | solution.py:106
  525.0 248.3 %all-reduce.5.cloned.1.call-start = ((), (), s32[]{:S(2)}) async-start(), calls=%async_computation.5 | async-start | bytes 3145728 | tf_op jit(solution)/shard_map/psum | solution.py:118
  773.3 5.3 copy-start.1
Sparse Core Ops, SparseCore 0:
  47.7 249.3 all-reduce.2
  536.3 236.9 all-reduce.4
where the time goes:
time: 796 us; the launch traced here: 786 us
  waiting for transfers between devices  537 us (67%)
  local copies, waits for them, and re-layouts  104 us (13%)
  other arithmetic  58 us (7%)
  matrix products  38.6 us (5%)
  starting transfers between devices  32.5 us (4%)
  between operations  15.5 us (2%)
    psum x1, waiting for transfers between devices, on_device(): lax.psum(back_sum.astype(jnp.bfloat16), 'seq').astype(jnp.float32)  196 us
    psum x1, waiting for transfers between devices, broadcast(): return lax.psum(kept, axis)  175 us
    ppermute x4, waiting for transfers between devices, passed_along(): return lax.ppermute(block, axis, route)  67.3 us
    all_to_all x1, waiting for transfers between devices, on_device(): lax.all_to_all(packed.reshape(1, block_rows, 2 * width_all), 'seq', split...  37.1 us
    all_to_all x1, waiting for transfers between devices, on_device(): lax.all_to_all(partner_terms.reshape(1, block_rows, 2 * width_all), 'seq'...  33.5 us
    all_to_all x1, waiting for transfers between devices, on_device(): lax.all_to_all(placed, 'seq', split_axis=0, concat_axis=1, tiled=True)  27.9 us
    unnamed x2, other arithmetic  25 us
    unnamed x32, local copies, waits for them, and re-layouts  24.5 us
  transfers between devices with their start and end apart: 10, of which 7 were waited for; matrix products, arithmetic and copies ran while one was open for 11% of the time, Pallas kernels for 0%

commit v1 on v0

v1 whole, which is shorter than its diff:
```python
import functools

import jax
import jax.numpy as jnp
from jax import lax
from jax.experimental import pallas as pl
from jax.experimental.pallas import tpu as pltpu
from jax.sharding import PartitionSpec as P

HEAD_DIM = 128
GLOBALS = 2
MESH = pl.DeviceIdType.MESH
LOG2E = 1.4426950408889634
F32, BF16 = jnp.float32, jnp.bfloat16


def matmul(a, b, ca, cb):
    return lax.dot_general(a, b, (((ca,), (cb,)), ((), ())), preferred_element_type=F32)


def kernel(
    groups, chips, rows,
    q_ref, k_ref, v_ref, g_ref, partner_ref, anchor_ref, list_ref,
    o_ref, dq_ref, dk_ref, dv_ref,
    kb, vb, qb, gb, ob, dqb, okt, ovt, pkt, pvt, dkb, dvb,
    kc, vc, live, bias, anchor_kv, gterm, gsend, grecv, gown, gother,
    in_send, in_recv, live_send, live_recv, local, swap_send, swap_recv,
    anchor_send, anchor_recv, out_send, out_recv, term_send, term_recv,
    gterm_send, gterm_recv, gswap_send, gswap_recv,
):
    seat, grp = lax.axis_index("seq"), lax.axis_index("grp")
    chip, core = lax.div(seat, 2), lax.rem(seat, 2)
    half = chips // 2
    scale = HEAD_DIM**-0.5
    mate = {"seq": chip * 2 + (1 - core)}

    def ring(n):
        return half + (2 * lax.rem(n, 2) - 1) * lax.div(n + 1, 2)

    def ahead(n):
        return lax.rem(chip + ring(n), chips)

    def behind(n):
        return lax.rem(chip - ring(n) + chips, chips)

    def columns(head):
        return pl.ds(pl.multiple_of(head * HEAD_DIM, HEAD_DIM), HEAD_DIM)

    def peer(other):
        return {"seq": other * 2 + core}

    def segment(offset):
        return {"grp": lax.rem(grp + offset + groups, groups)}

    def slot(block):
        return lax.div(block, 2) + chips * lax.rem(lax.rem(block, 2) + core, 2)

    def remote(src, dst, send, recv, device):
        return pltpu.make_async_remote_copy(
            src_ref=src, dst_ref=dst, send_sem=send, recv_sem=recv, device_id=device, device_id_type=MESH
        )

    inputs = ((k_ref, kb), (v_ref, vb), (q_ref, qb), (g_ref, gb))

    def bring(a, n):
        src, dst = inputs[a]
        to = ahead(n)
        return remote(src.at[:, columns(to)], dst.at[chip], in_send.at[a, n], in_recv.at[a, n], peer(to))

    def brought(a, n):
        src, dst = inputs[a]
        return remote(src.at[:, columns(chip)], dst.at[behind(n)], in_send.at[a, n], in_recv.at[a, n], peer(behind(n)))

    def own_in(a):
        src, dst = inputs[a]
        return pltpu.make_async_copy(src.at[:, columns(chip)], dst.at[chip], local.at[a])

    def show(n):
        return remote(live, bias.at[chip], live_send.at[n], live_recv.at[n], peer(ahead(n)))

    def shown(n):
        return remote(live, bias.at[behind(n)], live_send.at[n], live_recv.at[n], peer(behind(n)))

    outputs = ((ob, o_ref), (dqb, dq_ref), (dkb, dk_ref), (dvb, dv_ref))

    def give(a, n):
        src, dst = outputs[a]
        to = behind(n)
        return remote(src.at[to], dst.at[:, columns(chip)], out_send.at[a, n], out_recv.at[a, n], peer(to))

    def given(a, n):
        src, dst = outputs[a]
        come = ahead(n)
        return remote(src.at[chip], dst.at[:, columns(come)], out_send.at[a, n], out_recv.at[a, n], peer(come))

    def own_out(a):
        src, dst = outputs[a]
        return pltpu.make_async_copy(src.at[chip], dst.at[:, columns(chip)], local.at[4 + a])

    def swap(a, s):
        buf = (kb, vb)[a]
        return remote(buf.at[s], buf.at[chips + s], swap_send.at[a, s], swap_recv.at[a, s], mate)

    def swap_terms(a, s):
        buf = (pkt, pvt)[a]
        return remote(buf.at[s], buf.at[chips + s], term_send.at[a, s], term_recv.at[a, s], mate)

    def anchor_out(a, d):
        dst = (kc, vc)[a]
        return remote(
            anchor_kv.at[a], dst.at[pl.ds((1 + d) * rows, rows)], anchor_send.at[a, d - 1], anchor_recv.at[a, d - 1],
            segment(d),
        )

    def gterm_out(d):
        return remote(gsend.at[d - 1], grecv.at[d - 1], gterm_send.at[d - 1], gterm_recv.at[d - 1], segment(-d))

    def gswap():
        return remote(gown, gother, gswap_send.at[0], gswap_recv.at[0], mate)

    def loop(count, body):
        def step(n, carry):
            body(n)
            return carry

        lax.fori_loop(0, count, step, 0)

    listed = [
        jnp.where((list_ref[0, 0] == d) | (list_ref[0, 1] == d), 0.0, -jnp.inf).astype(F32) for d in (1, 2)
    ]
    lane = lax.broadcasted_iota(jnp.int32, live.shape, 1)
    live[...] = jnp.where(lane < rows, listed[0], listed[1])

    barrier = pltpu.get_barrier_semaphore()

    def greet(n):
        pl.semaphore_signal(barrier, inc=1, device_id=peer(ahead(n)), device_id_type=MESH)

    pl.semaphore_signal(barrier, inc=1, device_id=mate, device_id_type=MESH)
    loop(chips - 1, greet)
    for d in (1, 2, -1, -2):
        pl.semaphore_signal(barrier, inc=1, device_id=segment(d), device_id_type=MESH)
    pl.semaphore_wait(barrier, chips + 4)

    def send_kv(n):
        bring(0, n).start()
        bring(1, n).start()

    def send_qg(n):
        bring(2, n).start()
        bring(3, n).start()
        show(n).start()

    for a in range(4):
        own_in(a).start()
    loop(chips - 1, send_kv)
    loop(chips - 1, send_qg)
    bias[chip] = live[...]
    gterm[...] = jnp.zeros_like(gterm)

    for a in range(4):
        own_in(a).wait()
    for a in range(2):
        swap(a, chip).start()

    def pass_on(n):
        for a in range(2):
            brought(a, n).wait_recv()
            swap(a, behind(n)).start()

    loop(chips - 1, pass_on)

    def swapped(s):
        for a in range(2):
            swap(a, s).wait_recv()

    loop(chips, swapped)

    anchor = anchor_ref[0]
    anchor_kv[0] = kb[slot(anchor)]
    anchor_kv[1] = vb[slot(anchor)]
    for d in (1, 2):
        for a in range(2):
            anchor_out(a, d).start()
    for d in (1, 2):
        for a in range(2):
            anchor_out(a, d).wait_recv()

    def attend(i):
        n = lax.rem(i + chips - 1, chips)
        at = behind(n)

        @pl.when(i > 0)
        def _():
            brought(2, n).wait_recv()
            brought(3, n).wait_recv()
            shown(n).wait_recv()

        partner = slot(partner_ref[0, 2 * at + core])
        kc[pl.ds(0, rows)] = kb[at]
        kc[pl.ds(rows, rows)] = kb[partner]
        vc[pl.ds(0, rows)] = vb[at]
        vc[pl.ds(rows, rows)] = vb[partner]
        query, grad, keys, values = qb[at], gb[at], kc[...], vc[...]
        scores = matmul(query, keys, 1, 1)
        both, far = scores[:, : 2 * rows], scores[:, 2 * rows :] + bias[at][:1]
        scores = jnp.concatenate([both, far], 1)
        top = jnp.max(scores, axis=1, keepdims=True)
        lifted = jnp.exp2((scores - top) * (scale * LOG2E))
        probs = lifted * (1.0 / jnp.sum(lifted, axis=1, keepdims=True))
        weights = probs.astype(BF16)
        ob[at] = matmul(weights, values, 1, 0).astype(BF16)
        dprob = matmul(grad, values, 1, 1)
        delta = jnp.sum(probs * dprob, axis=1, keepdims=True)
        dscore = (probs * (dprob - delta)).astype(BF16)
        dqb[at] = (matmul(dscore, keys, 1, 0) * scale).astype(BF16)
        key_terms = matmul(dscore, query, 0, 0) * scale
        okt[at] = key_terms[:rows]
        pkt[at] = key_terms[rows : 2 * rows].astype(BF16)
        gterm[0] += key_terms[2 * rows :]
        value_terms = matmul(weights, grad, 0, 0)
        ovt[at] = value_terms[:rows]
        pvt[at] = value_terms[rows : 2 * rows].astype(BF16)
        gterm[1] += value_terms[2 * rows :]

        @pl.when(i > 0)
        def _():
            give(0, n).start()
            give(1, n).start()

        @pl.when(i == 0)
        def _():
            own_out(0).start()
            own_out(1).start()

        swap_terms(0, at).start()
        swap_terms(1, at).start()

    loop(chips, attend)

    for d in (1, 2):
        for a in range(2):
            gsend[d - 1, a] = gterm[a, (d - 1) * rows : d * rows].astype(BF16)
        gterm_out(d).start()
    for d in (1, 2):
        gterm_out(d).wait_recv()
    gown[...] = (grecv[0].astype(F32) + grecv[1].astype(F32)).astype(BF16)
    gswap().start()

    def terms_swapped(s):
        for a in range(2):
            swap_terms(a, s).wait_recv()

    loop(chips, terms_swapped)
    gswap().wait_recv()

    def finish(i):
        n = lax.rem(i + chips - 1, chips)
        at = behind(n)
        block = 2 * at + core
        source = jnp.int32(0)
        for s in range(2 * chips):
            source = jnp.where(partner_ref[0, s] == block, s, source)
        source = slot(source)
        here = jnp.where(anchor == block, 1.0, 0.0).astype(F32)
        for a, (own, far, out) in enumerate(((okt, pkt, dkb), (ovt, pvt, dvb))):
            back = grecv[0, a].astype(F32) + grecv[1, a].astype(F32) + gother[a].astype(F32)
            out[at] = (own[at] + far[source].astype(F32) + here * back).astype(BF16)

        @pl.when(i > 0)
        def _():
            give(2, n).start()
            give(3, n).start()

        @pl.when(i == 0)
        def _():
            own_out(2).start()
            own_out(3).start()

    loop(chips, finish)

    def sent(n):
        for a in range(4):
            bring(a, n).wait_send()
        show(n).wait_send()

    loop(chips - 1, sent)

    def swaps_sent(s):
        for a in range(2):
            swap(a, s).wait_send()
            swap_terms(a, s).wait_send()

    loop(chips, swaps_sent)
    for d in (1, 2):
        for a in range(2):
            anchor_out(a, d).wait_send()
        gterm_out(d).wait_send()
    gswap().wait_send()
    for a in range(4):
        own_out(a).wait()

    def done(n):
        for a in range(4):
            give(a, n).wait_send()
            given(a, n).wait_recv()

    loop(chips - 1, done)


def on_device(groups, seats, query_rows, key_rows, value_rows, cotangent, partner, anchors, global_list):
    rows, width = query_rows.shape
    chips = seats // 2
    hbm, anywhere = pl.BlockSpec(memory_space=pltpu.HBM), pl.BlockSpec(memory_space=pl.ANY)
    smem = pl.BlockSpec(memory_space=pltpu.SMEM)
    vmem, dma = pltpu.VMEM, pltpu.SemaphoreType.DMA
    piece = (rows, HEAD_DIM)
    wide = (GLOBALS * rows, HEAD_DIM)
    return pl.pallas_call(
        functools.partial(kernel, groups, chips, rows),
        out_shape=[jax.ShapeDtypeStruct((rows, width), BF16)] * 4,
        in_specs=[hbm] * 4 + [smem] * 3,
        out_specs=[anywhere] * 4,
        scratch_shapes=[
            vmem((2 * chips, *piece), BF16),
            vmem((2 * chips, *piece), BF16),
            vmem((chips, *piece), BF16),
            vmem((chips, *piece), BF16),
            vmem((chips, *piece), BF16),
            vmem((chips, *piece), BF16),
            vmem((chips, *piece), F32),
            vmem((chips, *piece), F32),
            vmem((2 * chips, *piece), BF16),
            vmem((2 * chips, *piece), BF16),
            vmem((chips, *piece), BF16),
            vmem((chips, *piece), BF16),
            vmem(((2 + GLOBALS) * rows, HEAD_DIM), BF16),
            vmem(((2 + GLOBALS) * rows, HEAD_DIM), BF16),
            vmem((8, GLOBALS * rows), F32),
            vmem((chips, 8, GLOBALS * rows), F32),
            vmem((2, *piece), BF16),
            vmem((2, *wide), F32),
            vmem((2, 2, *piece), BF16),
            vmem((2, 2, *piece), BF16),
            vmem((2, *piece), BF16),
            vmem((2, *piece), BF16),
            dma((4, chips)), dma((4, chips)),
            dma((chips,)), dma((chips,)),
            dma((8,)),
            dma((2, chips)), dma((2, chips)),
            dma((2, 2)), dma((2, 2)),
            dma((4, chips)), dma((4, chips)),
            dma((2, chips)), dma((2, chips)),
            dma((2,)), dma((2,)),
            dma((1,)), dma((1,)),
        ],
        compiler_params=pltpu.CompilerParams(
            collective_id=0, has_side_effects=True, vmem_limit_bytes=48 * 2**20
        ),
        cost_estimate=pl.CostEstimate(flops=3_700_000_000, bytes_accessed=6_300_000, transcendentals=2_400_000),
    )(query_rows, key_rows, value_rows, cotangent, partner, anchors, global_list)


def solution(mesh):
    rows = P(("grp", "seq"), None)
    return jax.shard_map(
        functools.partial(on_device, mesh.shape["grp"], mesh.shape["seq"]),
        mesh=mesh,
        in_specs=(rows, rows, rows, rows, P("grp", None), P("grp"), rows),
        out_specs=(rows, rows, rows, rows),
        check_vma=False,
    )
```

time: 796 us -> 165 us (0.21); the launches traced: 786 us -> 165 us
  waiting for transfers between devices: 537 us -> 0 us
  Pallas kernels: 0 us -> 156 us
  local copies, waits for them, and re-layouts: 104 us -> 6.92 us
  other arithmetic: 58 us -> 0 us
  matrix products: 38.6 us -> 0 us
  starting transfers between devices: 32.5 us -> 0 us
  between operations: 15.5 us -> 1.35 us
    psum x2 -> x0, waiting for transfers between devices: 371 us -> none  [the longest x1 196 us: on_device(): lax.psum(back_sum.astype(jnp.bfloat16), 'seq').astype(jnp.float32)]
    pallas_call x0 -> x1, Pallas kernels: none -> 156 us  [on_device(): pl.pallas_call(functools.partial(kernel, groups, chips, rows), out_shape=...]
    all_to_all x4 -> x0, waiting for transfers between devices: 98.6 us -> none  [the longest x1 37.1 us: on_device(): lax.all_to_all(packed.reshape(1, block_rows, 2 * width_all), 'seq', split...]
    ppermute x4 -> x0, waiting for transfers between devices: 67.3 us -> none  [passed_along(): return lax.ppermute(block, axis, route)]
    all_to_all x4 -> x0, local copies, waits for them, and re-layouts: 30.9 us -> none  [the longest x2 16 us: on_device(): lax.all_to_all(packed.reshape(1, block_rows, 2 * width_all), 'seq', split...]
    dot_general x5 -> x0, matrix products: 30 us -> none  [the longest x1 10.1 us: attend_block(): jnp.einsum('hqk,qhd->khd', weights, grad_heads, preferred_element_type=jn...]
    all_to_all x4 -> x0, starting transfers between devices: 27.3 us -> none  [the longest x1 11.2 us: on_device(): lax.all_to_all(packed.reshape(1, block_rows, 2 * width_all), 'seq', split...]
    unnamed x2 -> x0, other arithmetic: 25 us -> none
  transfers between devices with their start and end apart: 10 -> 0, of which waited for: 7 -> 0; matrix products, arithmetic and copies ran while one was open for 11% -> 0% of each run, Pallas kernels for 0% -> 0%
where the time goes in v1:
time: 165 us
  Pallas kernels  156 us (95%)
  local copies, waits for them, and re-layouts  6.92 us (4%)
    pallas_call x1, Pallas kernels, on_device(): pl.pallas_call(functools.partial(kernel, groups, chips, rows), out_shape=...  156 us
    unnamed x14, local copies, waits for them, and re-layouts  6.92 us

profile of v1, /device:TPU:1, one launch (start us, length us, event | category | flops | bytes accessed | tf_op | source)
XLA Modules:
  0.0 164.7 jit_solution(13058410681711078308)
XLA Ops:
  0.6 0.0 copy-start.4
  0.6 0.0 copy-start.3
  1.3 0.0 copy-done.4
  1.3 0.0 copy-done.3
  1.3 0.0 copy-start
  1.3 1.1 copy-done
  2.5 0.0 copy-start.1
  2.5 1.1 copy-done.1
  3.6 0.0 copy-start.2
  3.6 1.1 copy-done.2
  4.7 156.4 %shard_map.102 = (bf16[192,2048]{1,0:T(8,128)(2,1)S(1)}, bf16[192,2048]{1,0:T(8,128)(2,1)S(1)}, bf16[192,2048]{1,0:T(8,128)(2,1)S(1)}, bf16[192,2048]{1,0:T(8,128)(2,1)S(1)}) custom-call(bf16[192,2048]{1,0:T(8,128)(2,1)S(1)} %copy-done, bf16[192,2048]{1,0:T(8,128)(2,1)S(1)} %copy-done.1, bf16[192,2048]{1,0:T(8,128)(2,1)S(1)} %copy-done.2, ...), custom_call_target="tpu_custom_call" | custom-call | flops 3700000000 | bytes 6300000 | tf_op jit(solution)/shard_map/pallas_call | solution.py:319
  161.2 0.9 copy.16
  162.1 0.9 copy.17
  163.0 0.9 copy.18
  163.8 0.9 copy.19
Async XLA Ops:
  0.6 0.7 copy-start.4
  0.6 0.7 copy-start.3
  1.3 1.1 copy-start
  2.5 1.1 copy-start.1
  3.6 1.1 copy-start.2

commit v2 on v1

v2 whole, which is shorter than its diff:
```python
import functools

import jax
import jax.numpy as jnp
from jax import lax
from jax.experimental import pallas as pl
from jax.experimental.pallas import tpu as pltpu
from jax.sharding import PartitionSpec as P

HEAD_DIM = 128
GLOBALS = 2
MESH = pl.DeviceIdType.MESH
LOG2E = 1.4426950408889634
VMEM_LIMIT = 62 * 2**20
PARTS = 2
F32, BF16 = jnp.float32, jnp.bfloat16


def matmul(a, b, ca, cb):
    return lax.dot_general(a, b, (((ca,), (cb,)), ((), ())), preferred_element_type=F32)


def kernel(
    groups, chips, rows,
    q_ref, k_ref, v_ref, g_ref, partner_hbm, anchor_hbm, list_hbm,
    o_ref, dq_ref, dk_ref, dv_ref,
    partner_ref, anchor_ref, list_ref,
    kv, qg, odq, dkv, own_terms, terms, key_set, live, bias, anchor_kv, gterm, gsend, grecv, gown, gother,
    small, local, in_send, kv_recv, qg_recv, live_sem, swap_sem, term_sem, anchor_sem, out_send, out_recv,
    gterm_sem, gswap_sem,
):
    seat, grp = lax.axis_index("seq"), lax.axis_index("grp")
    chip, core = lax.div(seat, 2), lax.rem(seat, 2)
    half, others = chips // 2, chips - 1
    scale = HEAD_DIM**-0.5
    mate = {"seq": chip * 2 + (1 - core)}

    def ring(n):
        return half + (2 * lax.rem(n, 2) - 1) * lax.div(n + 1, 2)

    def ahead(n):
        return lax.rem(chip + ring(n), chips)

    def behind(n):
        return lax.rem(chip - ring(n) + chips, chips)

    def columns(head):
        return pl.ds(pl.multiple_of(head * HEAD_DIM, HEAD_DIM), HEAD_DIM)

    def peer(other):
        return {"seq": other * 2 + core}

    def segment(offset):
        return {"grp": lax.rem(grp + offset + groups, groups)}

    def slot(block):
        return lax.div(block, 2) + chips * lax.rem(lax.rem(block, 2) + core, 2)

    def remote(src, dst, send, recv, device):
        return pltpu.make_async_remote_copy(
            src_ref=src, dst_ref=dst, send_sem=send, recv_sem=recv, device_id=device, device_id_type=MESH
        )

    def take(ref, sem):
        pltpu.make_async_copy(ref, ref, sem).wait()

    def bring(refs, buf, send, recv, n):
        to = ahead(n)
        for a in range(2):
            remote(refs[a].at[:, columns(to)], buf.at[chip, a], send, recv.at[n], peer(to)).start()

    def give(buf, refs, sems, n):
        to = behind(n)
        for a in range(2):
            remote(buf.at[to, a], refs[a].at[:, columns(chip)], out_send.at[sems], out_recv.at[sems], peer(to)).start()

    def own_in(refs, buf, sem):
        return [pltpu.make_async_copy(refs[a].at[:, columns(chip)], buf.at[chip, a], local.at[sem + a]) for a in range(2)]

    def own_out(buf, refs, sem):
        return [pltpu.make_async_copy(buf.at[chip, a], refs[a].at[:, columns(chip)], local.at[sem + a]) for a in range(2)]

    def show(n):
        return remote(live, bias.at[chip], live_sem.at[0], live_sem.at[1], peer(ahead(n)))

    def swap(buf, sems, s):
        return remote(buf.at[s], buf.at[chips + s], sems.at[0], sems.at[1], mate)

    def anchor_out(a, d):
        dst = key_set.at[a, pl.ds((1 + d) * rows, rows)]
        return remote(anchor_kv.at[a], dst, anchor_sem.at[0], anchor_sem.at[1], segment(d))

    def gterm_out(d):
        return remote(gsend.at[d - 1], grecv.at[d - 1], gterm_sem.at[0], gterm_sem.at[1], segment(-d))

    def gswap():
        return remote(gown, gother, gswap_sem.at[0], gswap_sem.at[1], mate)

    def loop(count, body):
        def step(n, carry):
            body(n)
            return carry

        lax.fori_loop(0, count, step, 0)

    scalars = [
        pltpu.make_async_copy(src, dst, small.at[a])
        for a, (src, dst) in enumerate(((partner_hbm, partner_ref), (anchor_hbm, anchor_ref), (list_hbm, list_ref)))
    ]
    for copy in scalars:
        copy.start()
    inputs_kv, inputs_qg = (k_ref, v_ref), (q_ref, g_ref)
    for copy in own_in(inputs_kv, kv, 0) + own_in(inputs_qg, qg, 2):
        copy.start()

    barrier = pltpu.get_barrier_semaphore()

    def greet(n):
        pl.semaphore_signal(barrier, inc=1, device_id=peer(ahead(n)), device_id_type=MESH)

    pl.semaphore_signal(barrier, inc=1, device_id=mate, device_id_type=MESH)
    loop(others, greet)
    for d in (1, 2, -1, -2):
        pl.semaphore_signal(barrier, inc=1, device_id=segment(d), device_id_type=MESH)
    for copy in scalars:
        copy.wait()
    for d in (1, 2):
        listed = jnp.where((list_ref[0, 0] == d) | (list_ref[0, 1] == d), 0.0, -jnp.inf).astype(F32)
        live[d - 1 : d] = jnp.full((1, HEAD_DIM), listed)
    pl.semaphore_wait(barrier, chips + 4)

    loop(others, lambda n: show(n).start())
    loop(others, lambda n: bring(inputs_kv, kv, in_send.at[0], kv_recv, n))
    loop(others, lambda n: bring(inputs_qg, qg, in_send.at[1], qg_recv, n))
    bias[chip] = live[...]
    gterm[...] = jnp.zeros_like(gterm)

    for copy in own_in(inputs_kv, kv, 0):
        copy.wait()
    swap(kv, swap_sem, chip).start()

    def pass_on(n):
        take(kv.at[behind(n)], kv_recv.at[n])
        swap(kv, swap_sem, behind(n)).start()

    loop(others, pass_on)
    take(kv.at[pl.ds(chips, chips)], swap_sem.at[1])

    anchor = anchor_ref[0]
    anchor_kv[...] = kv[slot(anchor)]
    for d in (1, 2):
        for a in range(2):
            anchor_out(a, d).start()
    for copy in own_in(inputs_qg, qg, 2):
        copy.wait()
    take(bias.at[pl.ds(0, others)], live_sem.at[1])
    take(key_set.at[:, pl.ds(2 * rows, GLOBALS * rows)], anchor_sem.at[1])

    def attend(i):
        n = lax.rem(i + others, chips)
        at = behind(n)

        @pl.when(i > 0)
        def _():
            take(qg.at[at], qg_recv.at[n])

        partner = slot(partner_ref[0, 2 * at + core])
        key_set[:, pl.ds(0, rows)] = kv[at]
        key_set[:, pl.ds(rows, rows)] = kv[partner]
        query, grad, keys, values = qg[at, 0], qg[at, 1], key_set[0], key_set[1]
        scores = matmul(query, keys, 1, 1)
        lane = lax.broadcasted_iota(jnp.int32, (1, HEAD_DIM), 1)
        first, second = bias[at][:1], bias[at][1:]
        offsets = [
            first if at_lane + HEAD_DIM <= rows else second if at_lane >= rows else jnp.where(lane < rows - at_lane, first, second)
            for at_lane in range(0, GLOBALS * rows, HEAD_DIM)
        ]
        offset = jnp.concatenate(offsets, 1)[:, : GLOBALS * rows]
        scores = jnp.concatenate([scores[:, : 2 * rows], scores[:, 2 * rows :] + offset], 1)
        top = jnp.max(scores, axis=1, keepdims=True)
        lifted = jnp.exp2((scores - top) * (scale * LOG2E))
        probs = lifted * (1.0 / jnp.sum(lifted, axis=1, keepdims=True))
        weights = probs.astype(BF16)
        odq[at, 0] = matmul(weights, values, 1, 0).astype(BF16)
        dprob = matmul(grad, values, 1, 1)
        delta = jnp.sum(probs * dprob, axis=1, keepdims=True)
        dscore = (probs * (dprob - delta)).astype(BF16)
        odq[at, 1] = (matmul(dscore, keys, 1, 0) * scale).astype(BF16)
        for a, term in enumerate((matmul(dscore, query, 0, 0) * scale, matmul(weights, grad, 0, 0))):
            own_terms[at, a] = term[:rows]
            terms[at, a] = term[rows : 2 * rows].astype(BF16)
            gterm[a] += term[2 * rows :]

        @pl.when(i > 0)
        def _():
            give(odq, (o_ref, dq_ref), 0, n)

        @pl.when(i == 0)
        def _():
            for copy in own_out(odq, (o_ref, dq_ref), 0):
                copy.start()

        swap(terms, term_sem, at).start()

    loop(chips, attend)

    for d in (1, 2):
        for a in range(2):
            gsend[d - 1, a] = gterm[a, (d - 1) * rows : d * rows].astype(BF16)
        gterm_out(d).start()
    take(grecv, gterm_sem.at[1])
    gown[...] = (grecv[0].astype(F32) + grecv[1].astype(F32)).astype(BF16)
    gswap().start()
    take(terms.at[pl.ds(chips, chips)], term_sem.at[1])
    take(gother, gswap_sem.at[1])

    def finish(i):
        n = lax.rem(i + others, chips)
        at = behind(n)
        block = 2 * at + core
        source = jnp.int32(0)
        for s in range(2 * chips):
            source = jnp.where(partner_ref[0, s] == block, s, source)
        source = slot(source)
        here = jnp.where(anchor == block, 1.0, 0.0).astype(F32)
        back = grecv[0].astype(F32) + grecv[1].astype(F32) + gother[...].astype(F32)
        dkv[at] = (own_terms[at] + terms[source].astype(F32) + here * back).astype(BF16)

        @pl.when(i > 0)
        def _():
            give(dkv, (dk_ref, dv_ref), 1, n)

        @pl.when(i == 0)
        def _():
            for copy in own_out(dkv, (dk_ref, dv_ref), 2):
                copy.start()

    loop(chips, finish)

    for a, buf in enumerate((kv, qg)):
        take(buf.at[pl.ds(0, others)], in_send.at[a])
    take(bias.at[pl.ds(0, others)], live_sem.at[0])
    take(kv.at[pl.ds(0, chips)], swap_sem.at[0])
    take(terms.at[pl.ds(0, chips)], term_sem.at[0])
    take(key_set.at[:, pl.ds(2 * rows, GLOBALS * rows)], anchor_sem.at[0])
    take(gsend, gterm_sem.at[0])
    take(gown, gswap_sem.at[0])
    for copy in own_out(odq, (o_ref, dq_ref), 0) + own_out(dkv, (dk_ref, dv_ref), 2):
        copy.wait()
    for sems in range(2):
        take(odq.at[pl.ds(0, others)], out_send.at[sems])
        take(odq.at[pl.ds(0, others)], out_recv.at[sems])


def write_out(parts, *refs):
    held, arrive, leave = refs[8:]
    height = held.shape[1] // parts

    def each(make):
        return [make(a, pl.ds(p * height, height), a * parts + p) for p in range(parts) for a in range(4)]

    arriving = each(lambda a, at, n: pltpu.make_async_copy(refs[a].at[at], held.at[a, at], arrive.at[n]))
    leaving = each(lambda a, at, n: pltpu.make_async_copy(held.at[a, at], refs[4 + a].at[at], leave.at[n]))
    for copy in arriving:
        copy.start()
    for come, go in zip(arriving, leaving, strict=True):
        come.wait()
        go.start()
    for copy in leaving:
        copy.wait()


def on_device(groups, seats, query_rows, key_rows, value_rows, cotangent, partner, anchors, global_list):
    rows, width = query_rows.shape
    chips = seats // 2
    anywhere = pl.BlockSpec(memory_space=pl.ANY)
    vmem, smem, dma = pltpu.VMEM, pltpu.SMEM, pltpu.SemaphoreType.DMA
    piece = (rows, HEAD_DIM)
    pair = (2, *piece)
    results = pl.pallas_call(
        functools.partial(kernel, groups, chips, rows),
        out_shape=[jax.ShapeDtypeStruct((rows, width), BF16)] * 4,
        in_specs=[anywhere] * 7,
        out_specs=[anywhere] * 4,
        scratch_shapes=[
            smem(partner.shape, jnp.int32),
            smem(anchors.shape, jnp.int32),
            smem(global_list.shape, jnp.int32),
            vmem((2 * chips, *pair), BF16),
            vmem((chips, *pair), BF16),
            vmem((chips, *pair), BF16),
            vmem((chips, *pair), BF16),
            vmem((chips, *pair), F32),
            vmem((2 * chips, *pair), BF16),
            vmem((2, (2 + GLOBALS) * rows, HEAD_DIM), BF16),
            vmem((2, HEAD_DIM), F32),
            vmem((chips, 2, HEAD_DIM), F32),
            vmem(pair, BF16),
            vmem((2, GLOBALS * rows, HEAD_DIM), F32),
            vmem((GLOBALS, *pair), BF16),
            vmem((GLOBALS, *pair), BF16),
            vmem(pair, BF16),
            vmem(pair, BF16),
            dma((3,)),
            dma((4,)),
            dma((2,)),
            dma((chips - 1,)),
            dma((chips - 1,)),
            dma((2,)),
            dma((2,)),
            dma((2,)),
            dma((2,)),
            dma((2,)),
            dma((2,)),
            dma((2,)),
            dma((2,)),
        ],
        compiler_params=pltpu.CompilerParams(collective_id=0, has_side_effects=True, vmem_limit_bytes=VMEM_LIMIT),
        cost_estimate=pl.CostEstimate(flops=3_700_000_000, bytes_accessed=6_300_000, transcendentals=2_400_000),
    )(query_rows, key_rows, value_rows, cotangent, partner, anchors, global_list)
    return pl.pallas_call(
        functools.partial(write_out, PARTS),
        out_shape=[jax.ShapeDtypeStruct((rows, width), BF16)] * 4,
        in_specs=[anywhere] * 4,
        out_specs=[anywhere] * 4,
        scratch_shapes=[vmem((4, rows, width), BF16), dma((4 * PARTS,)), dma((4 * PARTS,))],
    )(*results)


def solution(mesh):
    rows = P(("grp", "seq"), None)
    return jax.shard_map(
        functools.partial(on_device, mesh.shape["grp"], mesh.shape["seq"]),
        mesh=mesh,
        in_specs=(rows, rows, rows, rows, P("grp", None), P("grp"), rows),
        out_specs=(rows, rows, rows, rows),
        check_vma=False,
    )
```

time: 165 us -> 153 us (0.927)
  local copies, waits for them, and re-layouts: 6.92 us -> 0 us
  Pallas kernels: 156 us -> 152 us
    pallas_call x1, Pallas kernels: 156 us -> 149 us  [on_device(): pl.pallas_call(functools.partial(kernel, groups, chips, rows), out_shape=...]
    unnamed x14 -> x0, local copies, waits for them, and re-layouts: 6.92 us -> none
    pallas_call x0 -> x1, Pallas kernels: none -> 2.79 us  [on_device(): pl.pallas_call(functools.partial(write_out, PARTS), out_shape=[jax.ShapeD...]
where the time goes in v2:
time: 153 us
  Pallas kernels  152 us (99%)
    pallas_call x1, Pallas kernels, on_device(): pl.pallas_call(functools.partial(kernel, groups, chips, rows), out_shape=...  149 us

profile of v2, /device:TPU:1, one launch (start us, length us, event | category | flops | bytes accessed | tf_op | source)
XLA Modules:
  0.0 153.0 jit_solution(13803924272820732836)
XLA Ops:
  1.3 149.0 %shard_map.102 = (bf16[192,2048]{1,0:T(8,128)(2,1)}, bf16[192,2048]{1,0:T(8,128)(2,1)}, bf16[192,2048]{1,0:T(8,128)(2,1)}, bf16[192,2048]{1,0:T(8,128)(2,1)}) custom-call(bf16[192,2048]{1,0:T(8,128)(2,1)} %q_ref.1, bf16[192,2048]{1,0:T(8,128)(2,1)} %k_ref.1, bf16[192,2048]{1,0:T(8,128)(2,1)} %v_ref.1, bf16[192,2048]{1,0:T(8,128)(2,1)} %g_ref.1, ...), custom_call_target="tpu_custom_call" | custom-call | flops 3700000000 | bytes 6300000 | tf_op jit(solution)/shard_map/pallas_call | solution.py:280
  150.3 2.8 %shard_map.103 = (bf16[192,2048]{1,0:T(8,128)(2,1)}, bf16[192,2048]{1,0:T(8,128)(2,1)}, bf16[192,2048]{1,0:T(8,128)(2,1)}, bf16[192,2048]{1,0:T(8,128)(2,1)}) custom-call(bf16[192,2048]{1,0:T(8,128)(2,1)} %get-tuple-element.8.refs_0_, bf16[192,2048]{1,0:T(8,128)(2,1)} %get-tuple-element.9.refs_1_, bf16[192,2048]{1,0:T(8,128)(2,1)} %get-tuple-element.10.refs_2_, ...), custom_call_target="tpu_custom_call" | custom-call | tf_op jit(solution)/shard_map/pallas_call | solution.py:321

commit v3 on v2

--- a/solution.py
+++ b/solution.py
@@ -214,8 +214,11 @@
     take(terms.at[pl.ds(chips, chips)], term_sem.at[1])
     take(gother, gswap_sem.at[1])
 
+    places = max(chips // 2, 1)
+    inner = lax.min(lax.div(lax.rem(lax.div(chip, 2) + 1, places), 2), 1)
+
     def finish(i):
-        n = lax.rem(i + others, chips)
+        n = lax.rem(lax.rem(i + (1 - inner) * (2 * chips - 2 * i), chips) + others, chips)
         at = behind(n)
         block = 2 * at + core
         source = jnp.int32(0)

time: 153 us -> 151 us (0.987); the launches traced: 153 us -> 149 us
  Pallas kernels: 152 us -> 148 us
    pallas_call x1, Pallas kernels: 149 us -> 145 us  [on_device(): pl.pallas_call(functools.partial(kernel, groups, chips, rows), out_shape=...]
where the time goes in v3:
time: 151 us; the launch traced here: 149 us
  Pallas kernels  148 us (98%)
    pallas_call x1, Pallas kernels, on_device(): pl.pallas_call(functools.partial(kernel, groups, chips, rows), out_shape=...  145 us

profile of v3, /device:TPU:1, one launch (start us, length us, event | category | flops | bytes accessed | tf_op | source)
XLA Modules:
  0.0 149.0 jit_solution(9568198745929281357)
XLA Ops:
  1.3 144.9 %shard_map.102 = (bf16[192,2048]{1,0:T(8,128)(2,1)}, bf16[192,2048]{1,0:T(8,128)(2,1)}, bf16[192,2048]{1,0:T(8,128)(2,1)}, bf16[192,2048]{1,0:T(8,128)(2,1)}) custom-call(bf16[192,2048]{1,0:T(8,128)(2,1)} %q_ref.1, bf16[192,2048]{1,0:T(8,128)(2,1)} %k_ref.1, bf16[192,2048]{1,0:T(8,128)(2,1)} %v_ref.1, bf16[192,2048]{1,0:T(8,128)(2,1)} %g_ref.1, ...), custom_call_target="tpu_custom_call" | custom-call | flops 3700000000 | bytes 6300000 | tf_op jit(solution)/shard_map/pallas_call | solution.py:283
  146.2 2.8 %shard_map.103 = (bf16[192,2048]{1,0:T(8,128)(2,1)}, bf16[192,2048]{1,0:T(8,128)(2,1)}, bf16[192,2048]{1,0:T(8,128)(2,1)}, bf16[192,2048]{1,0:T(8,128)(2,1)}) custom-call(bf16[192,2048]{1,0:T(8,128)(2,1)} %get-tuple-element.8.refs_0_, bf16[192,2048]{1,0:T(8,128)(2,1)} %get-tuple-element.9.refs_1_, bf16[192,2048]{1,0:T(8,128)(2,1)} %get-tuple-element.10.refs_2_, ...), custom_call_target="tpu_custom_call" | custom-call | tf_op jit(solution)/shard_map/pallas_call | solution.py:324

commit v4 on v3

--- a/solution.py
+++ b/solution.py
@@ -11,8 +11,7 @@
 GLOBALS = 2
 MESH = pl.DeviceIdType.MESH
 LOG2E = 1.4426950408889634
-VMEM_LIMIT = 62 * 2**20
-PARTS = 2
+VMEM_LIMIT = 507 * 2**20 // 10
 F32, BF16 = jnp.float32, jnp.bfloat16
 
 
@@ -255,21 +254,12 @@
         take(odq.at[pl.ds(0, others)], out_recv.at[sems])
 
 
-def write_out(parts, *refs):
-    held, arrive, leave = refs[8:]
-    height = held.shape[1] // parts
-
-    def each(make):
-        return [make(a, pl.ds(p * height, height), a * parts + p) for p in range(parts) for a in range(4)]
-
-    arriving = each(lambda a, at, n: pltpu.make_async_copy(refs[a].at[at], held.at[a, at], arrive.at[n]))
-    leaving = each(lambda a, at, n: pltpu.make_async_copy(held.at[a, at], refs[4 + a].at[at], leave.at[n]))
-    for copy in arriving:
+def write_out(*refs):
+    sems = refs[-1]
+    copies = [pltpu.make_async_copy(refs[a], refs[4 + a], sems.at[a]) for a in range(4)]
+    for copy in copies:
         copy.start()
-    for come, go in zip(arriving, leaving, strict=True):
-        come.wait()
-        go.start()
-    for copy in leaving:
+    for copy in copies:
         copy.wait()
 
 
@@ -322,11 +312,12 @@
         cost_estimate=pl.CostEstimate(flops=3_700_000_000, bytes_accessed=6_300_000, transcendentals=2_400_000),
     )(query_rows, key_rows, value_rows, cotangent, partner, anchors, global_list)
     return pl.pallas_call(
-        functools.partial(write_out, PARTS),
+        write_out,
         out_shape=[jax.ShapeDtypeStruct((rows, width), BF16)] * 4,
         in_specs=[anywhere] * 4,
         out_specs=[anywhere] * 4,
-        scratch_shapes=[vmem((4, rows, width), BF16), dma((4 * PARTS,)), dma((4 * PARTS,))],
+        scratch_shapes=[dma((4,))],
+        compiler_params=pltpu.CompilerParams(vmem_limit_bytes=2**20),
     )(*results)
 
 

time: 151 us -> 150 us (level)
  no operation moved by 1% of the time
where the time goes in v4:
time: 150 us; the launch traced here: 148 us
  Pallas kernels  147 us (98%)
    pallas_call x1, Pallas kernels, on_device(): pl.pallas_call(functools.partial(kernel, groups, chips, rows), out_shape=...  145 us

profile of v4, /device:TPU:1, one launch (start us, length us, event | category | flops | bytes accessed | tf_op | source)
XLA Modules:
  0.0 148.0 jit_solution(1097778806098598567)
XLA Ops:
  0.6 0.0 copy-start.1
  0.6 0.0 copy-start
  1.3 0.0 copy-done.1
  1.3 0.0 copy-done
  1.3 144.9 %shard_map.102 = (bf16[192,2048]{1,0:T(8,128)(2,1)S(1)}, bf16[192,2048]{1,0:T(8,128)(2,1)S(1)}, bf16[192,2048]{1,0:T(8,128)(2,1)S(1)}, bf16[192,2048]{1,0:T(8,128)(2,1)S(1)}) custom-call(bf16[192,2048]{1,0:T(8,128)(2,1)} %q_ref.1, bf16[192,2048]{1,0:T(8,128)(2,1)} %k_ref.1, bf16[192,2048]{1,0:T(8,128)(2,1)} %v_ref.1, bf16[192,2048]{1,0:T(8,128)(2,1)} %g_ref.1, ...), custom_call_target="tpu_custom_call" | custom-call | flops 3700000000 | bytes 6300000 | tf_op jit(solution)/shard_map/pallas_call | solution.py:273
  146.3 1.7 %shard_map.103 = (bf16[192,2048]{1,0:T(8,128)(2,1)}, bf16[192,2048]{1,0:T(8,128)(2,1)}, bf16[192,2048]{1,0:T(8,128)(2,1)}, bf16[192,2048]{1,0:T(8,128)(2,1)}) custom-call(bf16[192,2048]{1,0:T(8,128)(2,1)S(1)} %get-tuple-element.8.refs_0_, bf16[192,2048]{1,0:T(8,128)(2,1)S(1)} %get-tuple-element.9.refs_1_, bf16[192,2048]{1,0:T(8,128)(2,1)S(1)} %get-tuple-element.10.refs_2_, ...), custom_call_target="tpu_custom_call" | custom-call | tf_op jit(solution)/shard_map/pallas_call | solution.py:314
Async XLA Ops:
  0.6 0.7 copy-start.1
  0.6 0.7 copy-start

commit v5 on v4

--- a/solution.py
+++ b/solution.py
@@ -102,6 +102,15 @@
 
         lax.fori_loop(0, count, step, 0)
 
+    barrier = pltpu.get_barrier_semaphore()
+
+    def greet(n):
+        pl.semaphore_signal(barrier, inc=1, device_id=peer(ahead(n)), device_id_type=MESH)
+
+    pl.semaphore_signal(barrier, inc=1, device_id=mate, device_id_type=MESH)
+    loop(others, greet)
+    for d in (1, 2, -1, -2):
+        pl.semaphore_signal(barrier, inc=1, device_id=segment(d), device_id_type=MESH)
     scalars = [
         pltpu.make_async_copy(src, dst, small.at[a])
         for a, (src, dst) in enumerate(((partner_hbm, partner_ref), (anchor_hbm, anchor_ref), (list_hbm, list_ref)))
@@ -112,24 +121,15 @@
     for copy in own_in(inputs_kv, kv, 0) + own_in(inputs_qg, qg, 2):
         copy.start()
 
-    barrier = pltpu.get_barrier_semaphore()
-
-    def greet(n):
-        pl.semaphore_signal(barrier, inc=1, device_id=peer(ahead(n)), device_id_type=MESH)
-
-    pl.semaphore_signal(barrier, inc=1, device_id=mate, device_id_type=MESH)
-    loop(others, greet)
-    for d in (1, 2, -1, -2):
-        pl.semaphore_signal(barrier, inc=1, device_id=segment(d), device_id_type=MESH)
+    pl.semaphore_wait(barrier, chips + 4)
+
+    loop(others, lambda n: bring(inputs_kv, kv, in_send.at[0], kv_recv, n))
     for copy in scalars:
         copy.wait()
     for d in (1, 2):
         listed = jnp.where((list_ref[0, 0] == d) | (list_ref[0, 1] == d), 0.0, -jnp.inf).astype(F32)
         live[d - 1 : d] = jnp.full((1, HEAD_DIM), listed)
-    pl.semaphore_wait(barrier, chips + 4)
-
     loop(others, lambda n: show(n).start())
-    loop(others, lambda n: bring(inputs_kv, kv, in_send.at[0], kv_recv, n))
     loop(others, lambda n: bring(inputs_qg, qg, in_send.at[1], qg_recv, n))
     bias[chip] = live[...]
     gterm[...] = jnp.zeros_like(gterm)

time: 150 us -> 150 us (level)
  no operation moved by 1% of the time
where the time goes in v5:
time: 150 us; the launch traced here: 148 us
  Pallas kernels  146 us (97%)
    pallas_call x1, Pallas kernels, on_device(): pl.pallas_call(functools.partial(kernel, groups, chips, rows), out_shape=...  145 us

profile of v5, /device:TPU:1, one launch (start us, length us, event | category | flops | bytes accessed | tf_op | source)
XLA Modules:
  0.0 147.8 jit_solution(4327277819236519362)
XLA Ops:
  0.6 0.0 copy-start.1
  0.6 0.0 copy-start
  1.3 0.0 copy-done.1
  1.3 0.0 copy-done
  1.3 144.8 %shard_map.102 = (bf16[192,2048]{1,0:T(8,128)(2,1)S(1)}, bf16[192,2048]{1,0:T(8,128)(2,1)S(1)}, bf16[192,2048]{1,0:T(8,128)(2,1)S(1)}, bf16[192,2048]{1,0:T(8,128)(2,1)S(1)}) custom-call(bf16[192,2048]{1,0:T(8,128)(2,1)} %q_ref.1, bf16[192,2048]{1,0:T(8,128)(2,1)} %k_ref.1, bf16[192,2048]{1,0:T(8,128)(2,1)} %v_ref.1, bf16[192,2048]{1,0:T(8,128)(2,1)} %g_ref.1, ...), custom_call_target="tpu_custom_call" | custom-call | flops 3700000000 | bytes 6300000 | tf_op jit(solution)/shard_map/pallas_call | solution.py:273
  146.1 1.7 %shard_map.103 = (bf16[192,2048]{1,0:T(8,128)(2,1)}, bf16[192,2048]{1,0:T(8,128)(2,1)}, bf16[192,2048]{1,0:T(8,128)(2,1)}, bf16[192,2048]{1,0:T(8,128)(2,1)}) custom-call(bf16[192,2048]{1,0:T(8,128)(2,1)S(1)} %get-tuple-element.8.refs_0_, bf16[192,2048]{1,0:T(8,128)(2,1)S(1)} %get-tuple-element.9.refs_1_, bf16[192,2048]{1,0:T(8,128)(2,1)S(1)} %get-tuple-element.10.refs_2_, ...), custom_call_target="tpu_custom_call" | custom-call | tf_op jit(solution)/shard_map/pallas_call | solution.py:314
Async XLA Ops:
  0.6 0.7 copy-start.1
  0.6 0.7 copy-start
